TPU v7x, 32 devices: a whole 2x2x4 slice. The times are simulated.
32 devices in a mesh: dp: 8 (over z, core), fsdp: 4 (over y, x).
Axes of the slice: x: 2, y: 2, z: 4, core: 2. Of those that a mesh axis runs over, the one named last changes fastest.
Arguments:
- tokens: bfloat16 [1024, 3072], P('dp', 'fsdp'), may hold values from -6 to 6
- weight_blocks: bfloat16 [96, 3, 128, 128], P('fsdp'), may hold values from -0.3125 to 0.3125
- pattern: int32 [96, 3], P('fsdp'), may hold values from 0 to 23, as said below
- grad_out: bfloat16 [1024, 12288], P('dp', 'fsdp'), may hold values from -6 to 6
Outputs:
- projected: bfloat16 [1024, 12288], P('dp', 'fsdp')
- grad_tokens: bfloat16 [1024, 3072], P('dp', 'fsdp')
- grad_weight: float32 [96, 3, 16384], P('fsdp', None, 'dp')
Inputs may be any that keep to these rules, and one draw needn't show every extreme that they name: `pattern`: each block-column names 3 different block-rows; every block-row is named by exactly 12 block-columns.
All inputs are finite; a program needn't handle non-finite values.
Results may differ from a plain program's by a relative error of at most 0.001.
Values may be sent and summed in bfloat16 or wider, within the bound.
A program may use at most 64 MiB of HBM per device.

v0:
```python
import jax
import jax.numpy as jnp
from jax import lax
from jax.sharding import PartitionSpec as P


def on_device(tokens, weight_blocks, pattern, grad_out):
    count_rows = tokens.shape[0]
    columns, slots, block_size = (
        weight_blocks.shape[0],
        weight_blocks.shape[1],
        weight_blocks.shape[3],
    )
    whole = lax.all_gather(tokens, "fsdp", axis=1, tiled=True)
    width = whole.shape[1]
    row_blocks = width // block_size
    whole_rows = whole.reshape(count_rows, row_blocks, block_size)
    grad_cols = grad_out.reshape(count_rows, columns, block_size)
    row_ids = jnp.arange(row_blocks, dtype=jnp.int32)
    projected_sum = jnp.zeros((count_rows, columns, block_size), jnp.float32)
    partial_grads = jnp.zeros((count_rows, row_blocks, block_size), jnp.float32)
    slot_terms = []
    for slot in range(slots):
        selector = row_ids[:, None] == pattern[:, slot][None, :]
        picked_slot = jnp.einsum(
            "trb,rc->tcb",
            whole_rows,
            selector.astype(jnp.bfloat16),
            preferred_element_type=jnp.float32,
        ).astype(jnp.bfloat16)
        weight_slot = weight_blocks[:, slot]
        projected_sum = projected_sum + jnp.einsum(
            "tcb,cbo->tco", picked_slot, weight_slot, preferred_element_type=jnp.float32
        )
        backward_slot = jnp.einsum(
            "tco,cbo->tcb", grad_cols, weight_slot, preferred_element_type=jnp.float32
        )
        partial_grads = partial_grads + jnp.einsum(
            "tcb,rc->trb",
            backward_slot,
            selector.astype(jnp.float32),
            precision=lax.Precision.HIGHEST,
        )
        slot_terms.append(
            jnp.einsum(
                "tcb,tco->cbo", picked_slot, grad_cols, preferred_element_type=jnp.float32
            ).reshape(columns, block_size * block_size)
        )
    projected = projected_sum.astype(jnp.bfloat16).reshape(count_rows, columns * block_size)
    partial_grads = partial_grads.reshape(count_rows, width)
    grad_tokens = lax.psum_scatter(partial_grads, "fsdp", scatter_dimension=1, tiled=True).astype(
        jnp.bfloat16
    )
    scale_factor = 1.0 / jnp.sqrt(jnp.float32(count_rows * lax.axis_size("dp")))
    weight_terms = jnp.stack(slot_terms, axis=1)
    grad_weight = (
        lax.psum_scatter(weight_terms, "dp", scatter_dimension=2, tiled=True) * scale_factor
    )
    return (projected, grad_tokens, grad_weight)


def solution(mesh):
    placed = (P("dp", "fsdp"), P("fsdp", None, None, None), P("fsdp", None), P("dp", "fsdp"))
    return jax.shard_map(
        on_device,
        mesh=mesh,
        in_specs=placed,
        out_specs=(P("dp", "fsdp"), P("dp", "fsdp"), P("fsdp", None, "dp")),
        check_vma=False,
    )
```

profile of v0, /device:TPU:0, one launch (start us, length us, event | category | flops | bytes accessed | tf_op | source)
XLA Modules:
  0.0 140.0 jit_solution(5769208513125036785)
XLA Ops:
  7.2 0.0 copy-start
  7.2 0.0 copy-start.1
  7.2 0.0 reduce-scatter.3.cloned.1.call-start
  7.2 1.1 copy-done
  8.3 3.0 %fusion.15 = f32[24,128,128]{2,1,0:T(8,128)} fusion(bf16[24,3,128,128]{3,2,1,0:T(8,128)(2,1)} %param.5, bf16[128,3072]{1,0:T(8,128)(2,1)S(1)} %copy-done), kind=kOutput, calls=%fused_computation.20 | convolution fusion | flops 100663296 | bytes 3145728 | tf_op jit(solution)/shard_map/tco,cbo->tcb/dot_general | solution.py:35
  11.3 0.0 copy-done.1
  11.3 1.8 %fusion.13 = f32[24,128,128]{2,1,0:T(8,128)} fusion(bf16[24,3,128,128]{3,2,1,0:T(8,128)(2,1)S(1)} %copy-done.1, bf16[128,3072]{1,0:T(8,128)(2,1)S(1)} %copy-done), kind=kOutput, calls=%fused_computation.18 | convolution fusion | flops 100663296 | bytes 3145728 | tf_op jit(solution)/shard_map/tco,cbo->tcb/dot_general | solution.py:35
  13.1 0.0 copy-start.13
  13.1 1.8 %fusion.11 = f32[24,128,128]{2,1,0:T(8,128)} fusion(bf16[24,3,128,128]{3,2,1,0:T(8,128)(2,1)S(1)} %copy-done.1, bf16[128,3072]{1,0:T(8,128)(2,1)S(1)} %copy-done), kind=kOutput, calls=%fused_computation.16 | convolution fusion | flops 100663296 | bytes 3145728 | tf_op jit(solution)/shard_map/tco,cbo->tcb/dot_general | solution.py:35
  14.9 0.0 copy-done.13
  14.9 3.0 %copy.27 = f32[24,128,128]{1,0,2:T(8,128)} copy(f32[24,128,128]{2,1,0:T(8,128)} %fusion.15) | data formatting | bytes 3145728 | tf_op jit(solution)/shard_map/tco,cbo->tcb/dot_general | solution.py:35
  18.0 0.0 copy-start.8
  18.0 3.2 %copy.28 = f32[24,128,128]{1,0,2:T(8,128)} copy(f32[24,128,128]{2,1,0:T(8,128)} %fusion.13) | data formatting | bytes 3145728 | tf_op jit(solution)/shard_map/tco,cbo->tcb/dot_general | solution.py:35
  21.1 0.0 copy-done.8
  21.1 1.6 %copy.29 = f32[24,128,128]{1,0,2:T(8,128)} copy(f32[24,128,128]{2,1,0:T(8,128)S(1)} %copy-done.8) | data formatting | bytes 3145728 | tf_op jit(solution)/shard_map/tco,cbo->tcb/dot_general | solution.py:35
  22.7 0.0 copy-start.11
  22.8 2.4 %fusion.2 = f32[24,128,128]{2,0,1:T(8,128)S(1)} fusion(f32[24,128,128]{1,0,2:T(8,128)} %copy.28, s32[24]{0:T(128)S(1)} %get-tuple-element.8), kind=kOutput, calls=%fused_computation.4 | convolution fusion | flops 113246784 | bytes 3145824 | tf_op jit(solution)/shard_map/tcb,rc->trb/dot_general | solution.py:38
  25.1 0.0 copy-done.11
  25.1 0.0 copy-start.10
  25.2 0.8 fusion
  26.0 0.5 copy-done.10
  26.6 1.0 add_add_fusion
  27.6 1.5 %copy.64 = f32[16,8,24,128]{3,1,2,0:T(8,128)} copy(f32[16,8,24,128]{3,2,1,0:T(8,128)S(1)} %bitcast.114) | data formatting | bytes 3145728
  29.0 0.0 copy-start.12
  29.0 0.0 reduce-scatter.3.cloned.1.call-update
  29.1 0.0 reduce-scatter.5.cloned.1.call-start
  29.1 0.9 copy-done.12
  30.0 20.8 %all_gather.3 = bf16[128,3072]{1,0:T(8,128)(2,1)S(1)} all-gather(bf16[128,768]{1,0:T(8,128)(2,1)S(1)} %copy-done.12), channel_id=1, replica_groups=mesh['dp'=8,'fsdp'=4] {'fsdp'}, dimensions={1}, use_global_device_ids=true | all-gather | bytes 983040 | tf_op jit(solution)/shard_map/all_gather | solution.py:14
  50.8 0.2 copy.37
  51.0 0.4 fusion.10
  51.4 1.3 fusion.9
  52.7 0.5 copy.20
  53.2 0.0 copy-start.6
  53.2 1.9 %copy.18 = bf16[128,24,128]{0,2,1:T(8,128)(2,1)S(1)} copy(bf16[128,24,128]{2,1,0:T(8,128)(2,1)} %fusion.9) | data formatting | bytes 1572864 | tf_op jit(solution)/shard_map/convert_element_type | solution.py:30
  55.1 0.0 copy-start.3
  55.1 1.3 fusion.8
  56.4 1.6 %copy.16 = bf16[128,24,128]{0,2,1:T(8,128)(2,1)S(1)} copy(bf16[128,24,128]{2,1,0:T(8,128)(2,1)} %fusion.8) | data formatting | bytes 1572864 | tf_op jit(solution)/shard_map/convert_element_type | solution.py:30
  58.1 0.0 copy-start.5
  58.1 1.5 %fusion.21 = f32[24,128,128]{2,1,0:T(8,128)} fusion(bf16[128,24,128]{0,2,1:T(8,128)(2,1)S(1)} %copy.16, bf16[128,3072]{1,0:T(8,128)(2,1)S(1)} %copy-done), kind=kOutput, calls=%fused_computation.26 | convolution fusion | flops 100663296 | bytes 3145728 | tf_op jit(solution)/shard_map/tcb,tco->cbo/dot_general | solution.py:45
  59.6 0.0 copy-done.5
  59.6 2.7 %stack_reshape.9 = f32[24,1,16384]{2,0,1:T(8,128)} reshape(f32[24,128,128]{2,1,0:T(8,128)} %fusion.21) | data formatting | bytes 3145728 | tf_op jit(solution)/shard_map/stack;reshape | solution.py:55
  62.3 0.0 copy-done.6
  62.3 1.5 %fusion.17 = f32[24,128,128]{2,1,0:T(8,128)} fusion(bf16[128,24,128]{0,2,1:T(8,128)(2,1)S(1)} %copy.20, bf16[128,3072]{1,0:T(8,128)(2,1)S(1)} %copy-done), kind=kOutput, calls=%fused_computation.22 | convolution fusion | flops 100663296 | bytes 3145728 | tf_op jit(solution)/shard_map/tcb,tco->cbo/dot_general | solution.py:45
  63.8 2.6 %stack_reshape.11 = f32[24,1,16384]{2,0,1:T(8,128)} reshape(f32[24,128,128]{2,1,0:T(8,128)} %fusion.17) | data formatting | bytes 3145728 | tf_op jit(solution)/shard_map/stack;reshape | solution.py:55
  66.4 0.0 copy-done.3
  66.4 1.5 %fusion.19 = f32[24,128,128]{2,1,0:T(8,128)} fusion(bf16[128,24,128]{0,2,1:T(8,128)(2,1)S(1)} %copy.18, bf16[128,3072]{1,0:T(8,128)(2,1)S(1)} %copy-done), kind=kOutput, calls=%fused_computation.24 | convolution fusion | flops 100663296 | bytes 3145728 | tf_op jit(solution)/shard_map/tcb,tco->cbo/dot_general | solution.py:45
  67.9 0.0 copy-start.9
  67.9 2.8 %stack_reshape.10 = f32[24,1,16384]{2,0,1:T(8,128)} reshape(f32[24,128,128]{2,1,0:T(8,128)} %fusion.19) | data formatting | bytes 3145728 | tf_op jit(solution)/shard_map/stack;reshape | solution.py:55
  70.7 0.0 copy-done.9
  70.7 4.3 %pad_maximum_fusion = f32[24,3,16384]{2,0,1:T(8,128)} fusion(f32[24,1,16384]{2,0,1:T(8,128)} %stack_reshape.11, f32[24,1,16384]{2,0,1:T(8,128)} %stack_reshape.10, f32[24,1,16384]{2,0,1:T(8,128)S(1)} %copy-done.9), kind=kLoop, calls=%fused_computation | loop fusion | flops 2359296 | bytes 9437184 | tf_op jit(solution)/shard_map/stack | solution.py:55
  75.0 0.0 copy-start.2
  75.0 0.0 reduce-scatter.5.cloned.1.call-update
  75.0 1.6 %copy-done.2 = bf16[24,3,128,128]{3,2,1,0:T(8,128)(2,1)S(1)} copy-done((bf16[24,3,128,128]{3,2,1,0:T(8,128)(2,1)S(1)}, bf16[24,3,128,128]{3,2,1,0:T(8,128)(2,1)}, u32[]{:S(2)}) %copy-start.2) | copy-done | bytes 2359320
  76.7 0.0 copy-start.4
  76.7 1.6 %fusion.29 = f32[24,128,128]{1,2,0:T(8,128)S(1)} fusion(bf16[128,24,128]{0,2,1:T(8,128)(2,1)} %copy-done.5, bf16[24,3,128,128]{3,2,1,0:T(8,128)(2,1)S(1)} %copy-done.2), kind=kOutput, calls=%fused_computation.34 | convolution fusion | flops 100663296 | bytes 3145728 | tf_op jit(solution)/shard_map/tcb,cbo->tco/dot_general | solution.py:32
  78.3 0.0 copy-done.4
  78.3 0.0 copy-start.7
  78.3 0.4 fusion.26
  78.8 0.7 copy-done.7
  79.4 1.4 add_convert_fusion
  80.8 2.3 %copy.22 = bf16[128,3072]{1,0:T(8,128)(2,1)} copy(bf16[128,3072]{0,1:T(8,128)(2,1)} %bitcast.116) | data formatting | bytes 1572864
  83.1 1.7 %convert_element_type.41 = bf16[128,768]{1,0:T(8,128)(2,1)} convert(f32[128,768]{1,0:T(8,128)} %reduce-scatter.3.cloned.1.call-done) | non-fusion elementwise | flops 98304 | bytes 589824 | tf_op jit(solution)/shard_map/convert_element_type | solution.py:51
  84.8 46.4 %reduce-scatter.5.cloned.1.call-done = f32[24,3,2048]{2,0,1:T(8,128)} async-done(((f32[24,3,16384]{2,0,1:T(8,128)}), f32[24,3,2048]{2,0,1:T(8,128)}) %reduce-scatter.5.cloned.1.call-update) | async-done | bytes 589840 | tf_op jit(solution)/shard_map/reduce_scatter | solution.py:57
  131.2 1.9 %broadcast_multiply_fusion = f32[24,3,2048]{2,0,1:T(8,128)} fusion(f32[24,3,2048]{2,0,1:T(8,128)} %reduce-scatter.5.cloned.1.call-done), kind=kLoop, calls=%fused_computation.48 | loop fusion | flops 147456 | bytes 1179648 | tf_op jit(solution)/shard_map/mul | solution.py:57
  (2 shorter events, 0.0 us)
Async XLA Ops:
  7.2 1.1 copy-start
  7.2 4.1 %copy-start.1 = (bf16[24,3,128,128]{3,2,1,0:T(8,128)(2,1)S(1)}, bf16[24,3,128,128]{3,2,1,0:T(8,128)(2,1)}, u32[]{:S(2)}) copy-start(bf16[24,3,128,128]{3,2,1,0:T(8,128)(2,1)} %param.5) | copy-start | bytes 7077892
  7.2 75.9 %reduce-scatter.3.cloned.1.call-start = ((), (), s32[]{:S(2)}) async-start(), calls=%async_computation.2 | async-start | bytes 1966080 | tf_op jit(solution)/shard_map/reduce_scatter | solution.py:51
  13.1 1.8 %copy-start.13 = (s32[24,3]{0,1:T(4,128)S(1)}, s32[24,3]{0,1:T(4,128)}, u32[]{:S(2)}) copy-start(s32[24,3]{0,1:T(4,128)} %param.6) | copy-start | bytes 868
  18.0 3.2 %copy-start.8 = (f32[24,128,128]{2,1,0:T(8,128)S(1)}, f32[24,128,128]{2,1,0:T(8,128)}, u32[]{:S(2)}) copy-start(f32[24,128,128]{2,1,0:T(8,128)} %fusion.11) | copy-start | bytes 4718596
  22.7 2.4 %copy-start.11 = (f32[24,128,128]{1,0,2:T(8,128)S(1)}, f32[24,128,128]{1,0,2:T(8,128)}, u32[]{:S(2)}) copy-start(f32[24,128,128]{1,0,2:T(8,128)} %copy.29) | copy-start | bytes 4718596
  25.1 1.4 %copy-start.10 = (f32[24,128,128]{1,0,2:T(8,128)S(1)}, f32[24,128,128]{1,0,2:T(8,128)}, u32[]{:S(2)}) copy-start(f32[24,128,128]{1,0,2:T(8,128)} %copy.27) | copy-start | bytes 4718596
  29.0 0.9 copy-start.12
  29.1 102.2 %reduce-scatter.5.cloned.1.call-start = ((), (), s32[]{:S(2)}) async-start(), calls=%async_computation.3 | async-start | bytes 5308416 | tf_op jit(solution)/shard_map/reduce_scatter | solution.py:57
  53.2 9.1 %copy-start.6 = (bf16[128,24,128]{0,2,1:T(8,128)(2,1)}, bf16[128,24,128]{0,2,1:T(8,128)(2,1)S(1)}, u32[]{:S(2)}) copy-start(bf16[128,24,128]{0,2,1:T(8,128)(2,1)S(1)} %copy.20) | copy-start | bytes 2359300
  55.1 11.3 %copy-start.3 = (bf16[128,24,128]{0,2,1:T(8,128)(2,1)}, bf16[128,24,128]{0,2,1:T(8,128)(2,1)S(1)}, u32[]{:S(2)}) copy-start(bf16[128,24,128]{0,2,1:T(8,128)(2,1)S(1)} %copy.18) | copy-start | bytes 2359300
  58.1 1.5 %copy-start.5 = (bf16[128,24,128]{0,2,1:T(8,128)(2,1)}, bf16[128,24,128]{0,2,1:T(8,128)(2,1)S(1)}, u32[]{:S(2)}) copy-start(bf16[128,24,128]{0,2,1:T(8,128)(2,1)S(1)} %copy.16) | copy-start | bytes 2359300
  67.9 2.8 %copy-start.9 = (f32[24,1,16384]{2,0,1:T(8,128)S(1)}, f32[24,1,16384]{2,0,1:T(8,128)}, u32[]{:S(2)}) copy-start(f32[24,1,16384]{2,0,1:T(8,128)} %stack_reshape.9) | copy-start | bytes 4718596
  75.0 1.7 %copy-start.2 = (bf16[24,3,128,128]{3,2,1,0:T(8,128)(2,1)S(1)}, bf16[24,3,128,128]{3,2,1,0:T(8,128)(2,1)}, u32[]{:S(2)}) copy-start(bf16[24,3,128,128]{3,2,1,0:T(8,128)(2,1)} %param.5) | copy-start | bytes 7077892
  76.7 1.6 %copy-start.4 = (bf16[128,24,128]{0,2,1:T(8,128)(2,1)S(1)}, bf16[128,24,128]{0,2,1:T(8,128)(2,1)}, u32[]{:S(2)}) copy-start(bf16[128,24,128]{0,2,1:T(8,128)(2,1)} %copy-done.3) | copy-start | bytes 2359300
  78.3 1.1 copy-start.7
Sparse Core Ops, SparseCore 0:
  29.2 38.4 reduce-scatter.2
  75.1 56.0 reduce-scatter.4
where the time goes:
time: 141 us; the launch traced here: 140 us
  waiting for transfers between devices  46.5 us (33%)
  local copies, waits for them, and re-layouts  28.7 us (20%)
  matrix products  21.8 us (15%)
  blocking collectives  20.8 us (15%)
  between operations  14.2 us (10%)
  other arithmetic  7.92 us (6%)
    reduce_scatter x1, waiting for transfers between devices, on_device(): lax.psum_scatter(weight_terms, 'dp', scatter_dimension=2, tiled=True)  46.4 us
    all_gather x1, blocking collectives, on_device(): whole = lax.all_gather(tokens, 'fsdp', axis=1, tiled=True)  20.8 us
    unnamed x31, local copies, waits for them, and re-layouts  8.73 us
    another operation x3, local copies, waits for them, and re-layouts, on_device(): weight_terms = jnp.stack(slot_terms, axis=1)  8.1 us
    dot_general x3, local copies, waits for them, and re-layouts, on_device(): jnp.einsum('tco,cbo->tcb', grad_cols, weight_slot, preferred_element_type...  7.83 us
    dot_general x3, matrix products, on_device(): jnp.einsum('tco,cbo->tcb', grad_cols, weight_slot, preferred_element_type...  6.59 us
    dot_general x3, matrix products, on_device(): jnp.einsum('tcb,tco->cbo', picked_slot, grad_cols, preferred_element_type...  4.51 us
    another operation x1, other arithmetic, on_device(): weight_terms = jnp.stack(slot_terms, axis=1)  4.31 us
  transfers between devices with their start and end apart: 2, of which 1 were waited for; matrix products, arithmetic and copies ran while one was open for 23% of the time, Pallas kernels for 0%

commit v1 on v0

--- a/solution.py
+++ b/solution.py
@@ -1,10 +1,17 @@
+import functools
+
 import jax
 import jax.numpy as jnp
 from jax import lax
+from jax.experimental import pallas as pl
+from jax.experimental.pallas import tpu as pltpu
 from jax.sharding import PartitionSpec as P
 
-
-def on_device(tokens, weight_blocks, pattern, grad_out):
+MESH = pl.DeviceIdType.MESH
+LEVELS = 32766.0
+
+
+def plain(tokens, weight_blocks, pattern, grad_out):
     count_rows = tokens.shape[0]
     columns, slots, block_size = (
         weight_blocks.shape[0],
@@ -59,8 +66,277 @@
     return (projected, grad_tokens, grad_weight)
 
 
+def kernel(
+    nf, nz, group, factor,
+    pat, prev, tok, w_hbm, g_hbm,
+    out_p, out_t, out_w,
+    x_all, xb, xt, xt_sib, g_own, g_sib, w, acc, part, part_in, terms, q_out, q_in, s_out, s_in,
+    local_sem, ag_send, ag_recv, sib_send, sib_recv, rs_send, rs_recv, z_send, z_recv, s_send, s_recv,
+):
+    d = lax.axis_index("dp")
+    f = lax.axis_index("fsdp")
+    z = d // 2
+    core = lax.rem(d, 2)
+    sib = (z * 2 + 1 - core, f)
+    columns, slots, blk, _ = w.shape
+    entries = columns * slots
+    row_blocks = xb.shape[0]
+    per = row_blocks // nf
+    chunks = columns // group
+
+    def peer_f(j):
+        return lax.rem(f + j, nf)
+
+    def peer_z(j):
+        return lax.rem(z + j, nz)
+
+    local = [
+        pltpu.make_async_copy(g_hbm, g_own, local_sem.at[0]),
+        pltpu.make_async_copy(w_hbm, w, local_sem.at[1]),
+        pltpu.make_async_copy(tok, x_all.at[f], local_sem.at[2]),
+    ]
+    for copy in local:
+        copy.start()
+
+    barrier = pltpu.get_barrier_semaphore()
+    for j in range(1, nf):
+        pl.semaphore_signal(barrier, inc=1, device_id=(d, peer_f(j)), device_id_type=MESH)
+    for j in range(1, nz):
+        pl.semaphore_signal(
+            barrier, inc=1, device_id=(peer_z(j) * 2 + core, f), device_id_type=MESH
+        )
+    pl.semaphore_signal(barrier, inc=1, device_id=sib, device_id_type=MESH)
+    pl.semaphore_wait(barrier, nf + nz - 1)
+
+    gather = [
+        pltpu.make_async_remote_copy(
+            tok, x_all.at[f], ag_send.at[j - 1], ag_recv.at[j - 1],
+            device_id=(d, peer_f(j)), device_id_type=MESH,
+        )
+        for j in range(1, nf)
+    ]
+    for copy in gather:
+        copy.start()
+    g_swap = pltpu.make_async_remote_copy(
+        g_hbm, g_sib, sib_send.at[0], sib_recv.at[0], device_id=sib, device_id_type=MESH
+    )
+    g_swap.start()
+
+    acc[entries] = jnp.zeros((blk, blk), jnp.float32)
+    local[0].wait()
+    local[1].wait()
+
+    def lanes(c):
+        return pl.ds(pl.multiple_of(c * blk, blk), blk)
+
+    def backward(c):
+        terms_c = lax.dot_general(
+            g_own[:, lanes(c)], w[c].reshape(slots * blk, blk),
+            (((1,), (1,)), ((), ())), preferred_element_type=jnp.float32,
+        )
+        for k in range(slots):
+            e = c * slots + k
+            acc[e] = terms_c[:, k * blk:(k + 1) * blk] + acc[prev[e]]
+
+    @pl.loop(0, columns // 2)
+    def _(i):
+        backward(i * 2)
+        backward(i * 2 + 1)
+
+    for j in range(nf):
+        to = peer_f(j)
+        for i in range(per):
+            part[j, :, i * blk:(i + 1) * blk] = acc[prev[entries + to * per + i]]
+
+    local[2].wait()
+    for copy in gather:
+        copy.wait_recv()
+
+    scatter = [
+        pltpu.make_async_remote_copy(
+            part.at[j], part_in.at[j - 1], rs_send.at[j - 1], rs_recv.at[j - 1],
+            device_id=(d, peer_f(j)), device_id_type=MESH,
+        )
+        for j in range(1, nf)
+    ]
+    rows = xt.shape[3]
+    for r in range(row_blocks):
+        block = x_all[r // per, :, (r % per) * blk:(r % per + 1) * blk]
+        xb[r] = block
+        xt[r] = block.T.reshape(nz, 2, rows, blk)
+    x_swap = pltpu.make_async_remote_copy(
+        xt.at[:, :, 1 - core], xt_sib, sib_send.at[1], sib_recv.at[1],
+        device_id=sib, device_id_type=MESH,
+    )
+    x_swap.start()
+    for copy in scatter:
+        copy.start()
+    g_swap.wait_recv()
+    x_swap.wait_recv()
+
+    def z_copies(n, j):
+        where = (peer_z(j) * 2 + core, f)
+        return (
+            pltpu.make_async_remote_copy(
+                q_out.at[peer_z(j), n], q_in.at[j - 1, n],
+                z_send.at[j - 1, n], z_recv.at[j - 1, n],
+                device_id=where, device_id_type=MESH,
+            ),
+            pltpu.make_async_remote_copy(
+                s_out.at[peer_z(j), n], s_in.at[j - 1, n],
+                s_send.at[j - 1, n], s_recv.at[j - 1, n],
+                device_id=where, device_id_type=MESH,
+            ),
+        )
+
+    @pl.loop(0, chunks)
+    def _(n):
+        for i in range(group):
+            c = n * group + i
+            lhs = jnp.concatenate(
+                [
+                    jnp.concatenate(
+                        [
+                            xt[pat[c, k], :, core].reshape(nz * rows, blk),
+                            xt_sib[pat[c, k]].reshape(nz * rows, blk),
+                        ],
+                        axis=1,
+                    )
+                    for k in range(slots)
+                ],
+                axis=0,
+            )
+            rhs = jnp.concatenate([g_own[:, lanes(c)], g_sib[:, lanes(c)]], axis=0)
+            sums = jnp.dot(lhs, rhs, preferred_element_type=jnp.float32)
+            sums = sums.reshape(slots, nz, rows, blk)
+            for v in range(nz):
+                mine = sums[:, v]
+                terms[c, v] = mine
+                top = jnp.max(jnp.max(jnp.abs(mine), axis=0), axis=0, keepdims=True)
+                top = jnp.maximum(top, 1e-30)
+                s_out[v, n, i:i + 1] = top * (1.0 / LEVELS)
+                coded = jnp.round(mine * (LEVELS / top))
+                q_out[v, n, i] = coded.astype(jnp.int32).astype(jnp.int16)
+        for j in range(1, nz):
+            for copy in z_copies(n, j):
+                copy.start()
+
+    def forward(c):
+        lhs = jnp.concatenate([xb[pat[c, k]] for k in range(slots)], axis=1)
+        total = jnp.dot(
+            lhs, w[c].reshape(slots * blk, blk), preferred_element_type=jnp.float32
+        )
+        out_p[:, lanes(c)] = total.astype(out_p.dtype)
+
+    @pl.loop(0, columns // 2)
+    def _(i):
+        forward(i * 2)
+        forward(i * 2 + 1)
+
+    for copy in scatter:
+        copy.wait_recv()
+    total = part[0]
+    for j in range(nf - 1):
+        total = total + part_in[j]
+    out_t[...] = total.astype(out_t.dtype)
+
+    @pl.loop(0, chunks)
+    def _(n):
+        for j in range(1, nz):
+            for copy in z_copies(n, j):
+                copy.wait_recv()
+        for i in range(group):
+            c = n * group + i
+            total = terms[c, z]
+            for j in range(nz - 1):
+                coded = q_in[j, n, i].astype(jnp.int32).astype(jnp.float32)
+                total = total + coded * s_in[j, n, i:i + 1].reshape(1, 1, blk)
+            out_w[c] = total * factor
+
+    for copy in gather + scatter + [g_swap, x_swap]:
+        copy.wait_send()
+
+    @pl.loop(0, chunks)
+    def _(n):
+        for j in range(1, nz):
+            for copy in z_copies(n, j):
+                copy.wait_send()
+
+
+def fused(nd, nf, tokens, weight_blocks, pattern, grad_out):
+    count, width = tokens.shape
+    columns, slots, blk, _ = weight_blocks.shape
+    row_blocks = width * nf // blk
+    entries = columns * slots
+    nz = nd // 2
+    rows = blk // nd
+    group = 4
+    chunks = columns // group
+    flat = pattern.reshape(entries)
+    ids = jnp.arange(entries, dtype=jnp.int32)
+    keys = jnp.concatenate([flat, jnp.arange(row_blocks, dtype=jnp.int32)])
+    limit = jnp.concatenate([ids, jnp.full((row_blocks,), entries, jnp.int32)])
+    found = (flat[None, :] == keys[:, None]) & (ids[None, :] < limit[:, None])
+    last = jnp.max(jnp.where(found, ids[None, :], -1), axis=1)
+    prev = jnp.where(last < 0, entries, last)
+    vmem = pl.BlockSpec(memory_space=pltpu.VMEM)
+    smem = pl.BlockSpec(memory_space=pltpu.SMEM)
+    hbm = pl.BlockSpec(memory_space=pl.ANY)
+    dma = pltpu.SemaphoreType.DMA
+    bf, f32 = jnp.bfloat16, jnp.float32
+    projected, grad_tokens, grad_weight = pl.pallas_call(
+        functools.partial(kernel, nf, nz, group, float((count * nd) ** -0.5)),
+        out_shape=(
+            jax.ShapeDtypeStruct((count, columns * blk), bf),
+            jax.ShapeDtypeStruct((count, width), bf),
+            jax.ShapeDtypeStruct((columns, slots, rows, blk), f32),
+        ),
+        in_specs=[smem, smem, hbm, hbm, hbm],
+        out_specs=(vmem, vmem, vmem),
+        scratch_shapes=[
+            pltpu.VMEM((nf, count, width), bf),
+            pltpu.VMEM((row_blocks, count, blk), bf),
+            pltpu.VMEM((row_blocks, nz, 2, rows, count), bf),
+            pltpu.VMEM((row_blocks, nz, rows, count), bf),
+            pltpu.VMEM((count, columns * blk), bf),
+            pltpu.VMEM((count, columns * blk), bf),
+            pltpu.VMEM((columns, slots, blk, blk), bf),
+            pltpu.VMEM((entries + 1, count, blk), f32),
+            pltpu.VMEM((nf, count, width), f32),
+            pltpu.VMEM((nf - 1, count, width), f32),
+            pltpu.VMEM((columns, nz, slots, rows, blk), f32),
+            pltpu.VMEM((nz, chunks, group, slots, rows, blk), jnp.int16),
+            pltpu.VMEM((nz - 1, chunks, group, slots, rows, blk), jnp.int16),
+            pltpu.VMEM((nz, chunks, 8, blk), f32),
+            pltpu.VMEM((nz - 1, chunks, 8, blk), f32),
+            dma((3,)),
+            dma((nf - 1,)), dma((nf - 1,)),
+            dma((2,)), dma((2,)),
+            dma((nf - 1,)), dma((nf - 1,)),
+            dma((nz - 1, chunks)), dma((nz - 1, chunks)),
+            dma((nz - 1, chunks)), dma((nz - 1, chunks)),
+        ],
+        compiler_params=pltpu.CompilerParams(
+            collective_id=0, has_side_effects=True, vmem_limit_bytes=40 * 1024 * 1024
+        ),
+    )(pattern, prev, tokens, weight_blocks, grad_out)
+    return projected, grad_tokens, grad_weight.reshape(columns, slots, rows * blk)
+
+
 def solution(mesh):
+    nd, nf = mesh.shape["dp"], mesh.shape["fsdp"]
     placed = (P("dp", "fsdp"), P("fsdp", None, None, None), P("fsdp", None), P("dp", "fsdp"))
+
+    def on_device(tokens, weight_blocks, pattern, grad_out):
+        columns, slots, blk, _ = weight_blocks.shape
+        fits = (
+            nd % 2 == 0 and 4 <= nd and blk % (16 * nd) == 0 and blk == 128
+            and tokens.shape[0] == blk and columns % 4 == 0 and nf > 1
+        )
+        if fits:
+            return fused(nd, nf, tokens, weight_blocks, pattern, grad_out)
+        return plain(tokens, weight_blocks, pattern, grad_out)
+
     return jax.shard_map(
         on_device,
         mesh=mesh,

time: 141 us -> 55.7 us (0.40)
  waiting for transfers between devices: 46.5 us -> 0 us
  Pallas kernels: 0 us -> 46.1 us
  matrix products: 21.8 us -> 0 us
  local copies, waits for them, and re-layouts: 28.7 us -> 7.1 us
  blocking collectives: 20.8 us -> 0 us
  between operations: 14.2 us -> 0.67 us
  other arithmetic: 7.92 us -> 0.84 us
    reduce_scatter x2 -> x0, waiting for transfers between devices: 46.4 us -> none  [the longest x1 46.4 us: on_device(): lax.psum_scatter(weight_terms, 'dp', scatter_dimension=2, tiled=True)]
    pallas_call x0 -> x1, Pallas kernels: none -> 46.1 us  [fused(): pl.pallas_call(functools.partial(kernel, nf, nz, group, float((count * nd...]
    dot_general x15 -> x0, matrix products: 21.8 us -> none  [the longest x3 6.59 us: on_device(): jnp.einsum('tco,cbo->tcb', grad_cols, weight_slot, preferred_element_type...]
    all_gather x1 -> x0, blocking collectives: 20.8 us -> none  [on_device(): whole = lax.all_gather(tokens, 'fsdp', axis=1, tiled=True)]
    another operation x3 -> x0, local copies, waits for them, and re-layouts: 8.1 us -> none  [on_device(): weight_terms = jnp.stack(slot_terms, axis=1)]
    dot_general x3 -> x0, local copies, waits for them, and re-layouts: 7.83 us -> none  [on_device(): jnp.einsum('tco,cbo->tcb', grad_cols, weight_slot, preferred_element_type...]
    another operation x1 -> x0, other arithmetic: 4.31 us -> none  [on_device(): weight_terms = jnp.stack(slot_terms, axis=1)]
    convert_element_type x3 -> x0, local copies, waits for them, and re-layouts: 4.01 us -> none  [on_device(): picked_slot = jnp.einsum('trb,rc->tcb', whole_rows, selector.astype(jnp.b...]
  transfers between devices with their start and end apart: 2 -> 0, of which waited for: 1 -> 0; matrix products, arithmetic and copies ran while one was open for 23% -> 0% of each run, Pallas kernels for 0% -> 0%
where the time goes in v1:
time: 55.7 us; the launch traced here: 54.7 us
  Pallas kernels  46.1 us (83%)
  local copies, waits for them, and re-layouts  7.1 us (13%)
  other arithmetic  0.84 us (2%)
  between operations  0.67 us (1%)
    pallas_call x1, Pallas kernels, fused(): pl.pallas_call(functools.partial(kernel, nf, nz, group, float((count * nd...  46.1 us
    unnamed x9, local copies, waits for them, and re-layouts  6.04 us

profile of v1, /device:TPU:0, one launch (start us, length us, event | category | flops | bytes accessed | tf_op | source)
XLA Modules:
  0.0 54.7 jit_solution(17496617224472383565)
XLA Ops:
  0.6 0.8 %copy.14.pat = s32[24,3]{1,0:T(8,128)S(1)} copy(s32[24,3]{0,1:T(4,128)} %param.6) | data formatting | bytes 576 | tf_op args[2]
  1.4 0.1 eq.15
  1.5 0.1 pad_add_fusion
  1.6 0.8 %select_reduce_fusion = s32[96]{0:T(128)S(1)} fusion(s32[96]{0:T(128)} %constant.1.clone.1, s32[96]{0:T(128)S(1)} %pad_add_fusion, s32[72]{0:T(128)S(1)} %eq.15), kind=kLoop, calls=%fused_computation | loop fusion | flops 34464 | bytes 1440 | tf_op jit(solution)/shard_map/reduce_max | solution.py:280
  2.3 0.0 copy-start
  2.4 1.7 %copy-done = bf16[24,3,128,128]{3,2,1,0:T(8,128)(2,1)S(1)} copy-done((bf16[24,3,128,128]{3,2,1,0:T(8,128)(2,1)S(1)}, bf16[24,3,128,128]{3,2,1,0:T(8,128)(2,1)}, u32[]{:S(2)}) %copy-start) | copy-done | bytes 2359320
  4.0 0.0 copy-start.1
  4.0 1.1 %copy-done.1 = bf16[128,3072]{1,0:T(8,128)(2,1)S(1)} copy-done((bf16[128,3072]{1,0:T(8,128)(2,1)S(1)}, bf16[128,3072]{1,0:T(8,128)(2,1)}, u32[]{:S(2)}) %copy-start.1) | copy-done | bytes 786456
  5.1 0.0 copy-start.2
  5.1 0.9 %copy-done.2 = bf16[128,768]{1,0:T(8,128)(2,1)S(1)} copy-done((bf16[128,768]{1,0:T(8,128)(2,1)S(1)}, bf16[128,768]{1,0:T(8,128)(2,1)}, u32[]{:S(2)}) %copy-start.2) | copy-done | bytes 196632
  6.1 46.1 %shard_map.67 = (bf16[128,3072]{1,0:T(8,128)(2,1)S(1)}, bf16[128,768]{1,0:T(8,128)(2,1)S(1)}, f32[24,3,16,128]{3,2,1,0:T(8,128)S(1)}) custom-call(s32[24,3]{1,0:T(8,128)S(1)} %copy.14.pat, s32[96]{0:T(128)S(1)} %compare_select_fusion.prev, bf16[128,768]{1,0:T(8,128)(2,1)S(1)} %copy-done.2, bf16[24,3,128,128]{3,2,1,0:T(8,128)(2,1)S(1)} %copy-done, ...), custom_call_target="tpu_custom_call" | custom-call | tf_op jit(solution)/shard_map/pallas_call | solution.py:287
  52.2 0.1 copy.15
  52.3 0.9 %reshape.13 = f32[24,3,2048]{2,0,1:T(8,128)} reshape(f32[24,3,16,128]{3,2,0,1:T(8,128)S(1)} %copy.15) | data formatting | bytes 1179648 | tf_op jit(solution)/shard_map/reshape | solution.py:323
  53.2 0.9 %copy.18 = bf16[128,3072]{1,0:T(8,128)(2,1)} copy(bf16[128,3072]{1,0:T(8,128)(2,1)S(1)} %get-tuple-element.15) | data formatting | bytes 1572864
  54.1 0.7 %copy.19 = bf16[128,768]{1,0:T(8,128)(2,1)} copy(bf16[128,768]{1,0:T(8,128)(2,1)S(1)} %get-tuple-element.16) | data formatting | bytes 393216
  (2 shorter events, 0.0 us)
Async XLA Ops:
  2.3 1.7 %copy-start = (bf16[24,3,128,128]{3,2,1,0:T(8,128)(2,1)S(1)}, bf16[24,3,128,128]{3,2,1,0:T(8,128)(2,1)}, u32[]{:S(2)}) copy-start(bf16[24,3,128,128]{3,2,1,0:T(8,128)(2,1)} %w_hbm.1) | copy-start | bytes 7077892
  4.0 1.1 %copy-start.1 = (bf16[128,3072]{1,0:T(8,128)(2,1)S(1)}, bf16[128,3072]{1,0:T(8,128)(2,1)}, u32[]{:S(2)}) copy-start(bf16[128,3072]{1,0:T(8,128)(2,1)} %g_hbm.1) | copy-start | bytes 2359300
  5.1 0.9 %copy-start.2 = (bf16[128,768]{1,0:T(8,128)(2,1)S(1)}, bf16[128,768]{1,0:T(8,128)(2,1)}, u32[]{:S(2)}) copy-start(bf16[128,768]{1,0:T(8,128)(2,1)} %tok.1) | copy-start | bytes 589828

commit v2 on v1

--- a/solution.py
+++ b/solution.py
@@ -217,7 +217,7 @@
                 s_out[v, n, i:i + 1] = top * (1.0 / LEVELS)
                 coded = jnp.round(mine * (LEVELS / top))
                 q_out[v, n, i] = coded.astype(jnp.int32).astype(jnp.int16)
-        for j in range(1, nz):
+        for j in sorted(range(1, nz), key=lambda j: abs(2 * j - nz)):
             for copy in z_copies(n, j):
                 copy.start()
 
@@ -317,7 +317,7 @@
             dma((nz - 1, chunks)), dma((nz - 1, chunks)),
         ],
         compiler_params=pltpu.CompilerParams(
-            collective_id=0, has_side_effects=True, vmem_limit_bytes=40 * 1024 * 1024
+            collective_id=0, has_side_effects=True, vmem_limit_bytes=60 * 1024 * 1024
         ),
     )(pattern, prev, tokens, weight_blocks, grad_out)
     return projected, grad_tokens, grad_weight.reshape(columns, slots, rows * blk)

time: 55.7 us -> 54.7 us (0.982)
  local copies, waits for them, and re-layouts: 7.1 us -> 4.52 us
  Pallas kernels: 46.1 us -> 47.3 us
    unnamed x9, local copies, waits for them, and re-layouts: 6.04 us -> 2.33 us
    pallas_call x1, Pallas kernels: 46.1 us -> 47.3 us  [fused(): pl.pallas_call(functools.partial(kernel, nf, nz, group, float((count * nd...]
    pallas_call x1, local copies, waits for them, and re-layouts: 0.05 us -> 1.19 us  [fused(): pl.pallas_call(functools.partial(kernel, nf, nz, group, float((count * nd...]
where the time goes in v2:
time: 54.7 us; the launch traced here: 53.9 us
  Pallas kernels  47.3 us (86%)
  local copies, waits for them, and re-layouts  4.52 us (8%)
  other arithmetic  1.35 us (2%)
  between operations  0.68 us (1%)
    pallas_call x1, Pallas kernels, fused(): pl.pallas_call(functools.partial(kernel, nf, nz, group, float((count * nd...  47.3 us
    unnamed x9, local copies, waits for them, and re-layouts  2.33 us
    pallas_call x1, local copies, waits for them, and re-layouts, fused(): pl.pallas_call(functools.partial(kernel, nf, nz, group, float((count * nd...  1.19 us

profile of v2, /device:TPU:0, one launch (start us, length us, event | category | flops | bytes accessed | tf_op | source)
XLA Modules:
  0.0 53.9 jit_solution(2931055977413679800)
XLA Ops:
  0.6 0.8 %copy.14.pat = s32[24,3]{1,0:T(8,128)S(1)} copy(s32[24,3]{0,1:T(4,128)} %param.6) | data formatting | bytes 576 | tf_op args[2]
  1.4 0.0 copy-start.2
  1.4 0.1 eq.15
  1.5 0.1 pad_add_fusion
  1.6 0.8 %select_reduce_fusion = s32[96]{0:T(128)S(1)} fusion(s32[96]{0:T(128)} %constant.1.clone.1, s32[96]{0:T(128)S(1)} %pad_add_fusion, s32[72]{0:T(128)S(1)} %eq.15), kind=kLoop, calls=%fused_computation | loop fusion | flops 34464 | bytes 1440 | tf_op jit(solution)/shard_map/reduce_max | solution.py:280
  2.3 0.5 compare_select_fusion.prev
  2.8 0.0 copy-done.2
  2.9 47.3 %shard_map.67 = (bf16[128,3072]{1,0:T(8,128)(2,1)}, bf16[128,768]{1,0:T(8,128)(2,1)}, f32[24,3,16,128]{3,2,1,0:T(8,128)}) custom-call(s32[24,3]{1,0:T(8,128)} %copy-done.2, s32[96]{0:T(128)} %compare_select_fusion.prev, bf16[128,768]{1,0:T(8,128)(2,1)} %tok.1, bf16[24,3,128,128]{3,2,1,0:T(8,128)(2,1)} %w_hbm.1, bf16[128,3072]{1,0:T(8,128)(2,1)} %g_hbm.1), custom_call_target="tpu_custom_call" | custom-call | tf_op jit(solution)/shard_map/pallas_call | solution.py:287
  50.2 0.0 copy-start
  50.2 0.0 copy-start.1
  50.2 1.2 %copy.15 = f32[24,3,16,128]{3,2,0,1:T(8,128)S(1)} copy(f32[24,3,16,128]{3,2,1,0:T(8,128)} %get-tuple-element.8) | data formatting | bytes 1179648 | tf_op jit(solution)/shard_map/pallas_call | solution.py:287
  51.4 0.9 %reshape.13 = f32[24,3,2048]{2,0,1:T(8,128)} reshape(f32[24,3,16,128]{3,2,0,1:T(8,128)S(1)} %copy.15) | data formatting | bytes 1179648 | tf_op jit(solution)/shard_map/reshape | solution.py:323
  52.3 0.0 copy-done
  52.3 0.9 %copy.18 = bf16[128,3072]{1,0:T(8,128)(2,1)} copy(bf16[128,3072]{1,0:T(8,128)(2,1)S(1)} %copy-done) | data formatting | bytes 1572864
  53.2 0.0 copy-done.1
  53.2 0.7 %copy.19 = bf16[128,768]{1,0:T(8,128)(2,1)} copy(bf16[128,768]{1,0:T(8,128)(2,1)S(1)} %copy-done.1) | data formatting | bytes 393216
  (1 shorter events, 0.0 us)
Async XLA Ops:
  1.4 1.4 %copy-start.2 = (s32[24,3]{1,0:T(8,128)}, s32[24,3]{1,0:T(8,128)S(1)}, u32[]{:S(2)}) copy-start(s32[24,3]{1,0:T(8,128)S(1)} %copy.14.pat) | copy-start | bytes 868
  50.2 2.1 %copy-start = (bf16[128,3072]{1,0:T(8,128)(2,1)S(1)}, bf16[128,3072]{1,0:T(8,128)(2,1)}, u32[]{:S(2)}) copy-start(bf16[128,3072]{1,0:T(8,128)(2,1)} %get-tuple-element.15) | copy-start | bytes 2359300
  50.2 3.0 %copy-start.1 = (bf16[128,768]{1,0:T(8,128)(2,1)S(1)}, bf16[128,768]{1,0:T(8,128)(2,1)}, u32[]{:S(2)}) copy-start(bf16[128,768]{1,0:T(8,128)(2,1)} %get-tuple-element.16) | copy-start | bytes 589828

commit v3 on v2

--- a/solution.py
+++ b/solution.py
@@ -70,8 +70,9 @@
     nf, nz, group, factor,
     pat, prev, tok, w_hbm, g_hbm,
     out_p, out_t, out_w,
-    x_all, xb, xt, xt_sib, g_own, g_sib, w, acc, part, part_in, terms, q_out, q_in, s_out, s_in,
+    x_all, xb, xt, xt_sib, g_own, g_sib, w, acc, part, part_in, terms, q_out, q_in, s_out, s_in, q_mid, s_mid,
     local_sem, ag_send, ag_recv, sib_send, sib_recv, rs_send, rs_recv, z_send, z_recv, s_send, s_recv,
+    m_send, m_recv,
 ):
     d = lax.axis_index("dp")
     f = lax.axis_index("fsdp")
@@ -188,6 +189,25 @@
                 device_id=where, device_id_type=MESH,
             ),
         )
+
+    beside = 1 + z // (nz - 1)
+    ends = ((z == 0, (2, 1)), (z == nz - 1, (2, 3)))
+    inner = jnp.logical_and(z > 0, z < nz - 1)
+
+    def mid_copies(n):
+        return tuple(
+            pltpu.make_async_remote_copy(
+                out.at[nz - 1 - z, n], there.at[n], m_send.at[n, a], m_recv.at[n, a],
+                device_id=(beside * 2 + core, f), device_id_type=MESH,
+            )
+            for a, (out, there) in enumerate(((q_out, q_mid), (s_out, s_mid)))
+        )
+
+    def code(mine, v, n, i):
+        top = jnp.max(jnp.max(jnp.abs(mine), axis=0), axis=0, keepdims=True)
+        top = jnp.maximum(top, 1e-30)
+        s_out[v, n, i:i + 1] = top * (1.0 / LEVELS)
+        q_out[v, n, i] = jnp.round(mine * (LEVELS / top)).astype(jnp.int32).astype(jnp.int16)
 
     @pl.loop(0, chunks)
     def _(n):
@@ -212,14 +232,22 @@
             for v in range(nz):
                 mine = sums[:, v]
                 terms[c, v] = mine
-                top = jnp.max(jnp.max(jnp.abs(mine), axis=0), axis=0, keepdims=True)
-                top = jnp.maximum(top, 1e-30)
-                s_out[v, n, i:i + 1] = top * (1.0 / LEVELS)
-                coded = jnp.round(mine * (LEVELS / top))
-                q_out[v, n, i] = coded.astype(jnp.int32).astype(jnp.int16)
-        for j in sorted(range(1, nz), key=lambda j: abs(2 * j - nz)):
-            for copy in z_copies(n, j):
-                copy.start()
+                code(mine, v, n, i)
+
+        for here, js in ends:
+            @pl.when(here)
+            def _():
+                for copy in mid_copies(n):
+                    copy.start()
+                for j in js:
+                    for copy in z_copies(n, j):
+                        copy.start()
+
+        @pl.when(inner)
+        def _():
+            for j in (1, 3):
+                for copy in z_copies(n, j):
+                    copy.start()
 
     def forward(c):
         lhs = jnp.concatenate([xb[pat[c, k]] for k in range(slots)], axis=1)
@@ -228,10 +256,22 @@
         )
         out_p[:, lanes(c)] = total.astype(out_p.dtype)
 
-    @pl.loop(0, columns // 2)
-    def _(i):
-        forward(i * 2)
-        forward(i * 2 + 1)
+    @pl.loop(0, chunks)
+    def _(n):
+        for i in range(group):
+            forward(n * group + i)
+
+        @pl.when(inner)
+        def _():
+            for copy in mid_copies(n):
+                copy.wait_recv()
+            to = peer_z(2)
+            for i in range(group):
+                came = q_mid[n, i].astype(jnp.int32).astype(jnp.float32)
+                came = came * s_mid[n, i:i + 1].reshape(1, 1, blk)
+                code(terms[n * group + i, to] + came, to, n, i)
+            for copy in z_copies(n, 2):
+                copy.start()
 
     for copy in scatter:
         copy.wait_recv()
@@ -240,27 +280,44 @@
         total = total + part_in[j]
     out_t[...] = total.astype(out_t.dtype)
 
-    @pl.loop(0, chunks)
-    def _(n):
-        for j in range(1, nz):
+    def finish(n, js):
+        for j in js:
             for copy in z_copies(n, j):
                 copy.wait_recv()
         for i in range(group):
             c = n * group + i
             total = terms[c, z]
-            for j in range(nz - 1):
-                coded = q_in[j, n, i].astype(jnp.int32).astype(jnp.float32)
-                total = total + coded * s_in[j, n, i:i + 1].reshape(1, 1, blk)
+            for j in js:
+                coded = q_in[j - 1, n, i].astype(jnp.int32).astype(jnp.float32)
+                total = total + coded * s_in[j - 1, n, i:i + 1].reshape(1, 1, blk)
             out_w[c] = total * factor
+
+    for here, js in ((z == 0, (2, 3)), (z == nz - 1, (1, 2)), (inner, (1, 2, 3))):
+        @pl.when(here)
+        def _():
+            @pl.loop(0, chunks)
+            def _(n):
+                finish(n, js)
 
     for copy in gather + scatter + [g_swap, x_swap]:
         copy.wait_send()
 
     @pl.loop(0, chunks)
     def _(n):
-        for j in range(1, nz):
-            for copy in z_copies(n, j):
-                copy.wait_send()
+        for here, js in ends:
+            @pl.when(here)
+            def _():
+                for copy in mid_copies(n):
+                    copy.wait_send()
+                for j in js:
+                    for copy in z_copies(n, j):
+                        copy.wait_send()
+
+        @pl.when(inner)
+        def _():
+            for j in (1, 2, 3):
+                for copy in z_copies(n, j):
+                    copy.wait_send()
 
 
 def fused(nd, nf, tokens, weight_blocks, pattern, grad_out):
@@ -309,12 +366,15 @@
             pltpu.VMEM((nz - 1, chunks, group, slots, rows, blk), jnp.int16),
             pltpu.VMEM((nz, chunks, 8, blk), f32),
             pltpu.VMEM((nz - 1, chunks, 8, blk), f32),
+            pltpu.VMEM((chunks, group, slots, rows, blk), jnp.int16),
+            pltpu.VMEM((chunks, 8, blk), f32),
             dma((3,)),
             dma((nf - 1,)), dma((nf - 1,)),
             dma((2,)), dma((2,)),
             dma((nf - 1,)), dma((nf - 1,)),
             dma((nz - 1, chunks)), dma((nz - 1, chunks)),
             dma((nz - 1, chunks)), dma((nz - 1, chunks)),
+            dma((chunks, 2)), dma((chunks, 2)),
         ],
         compiler_params=pltpu.CompilerParams(
             collective_id=0, has_side_effects=True, vmem_limit_bytes=60 * 1024 * 1024
@@ -330,7 +390,7 @@
     def on_device(tokens, weight_blocks, pattern, grad_out):
         columns, slots, blk, _ = weight_blocks.shape
         fits = (
-            nd % 2 == 0 and 4 <= nd and blk % (16 * nd) == 0 and blk == 128
+            nd == 8 and blk == 128
             and tokens.shape[0] == blk and columns % 4 == 0 and nf > 1
         )
         if fits:

time: 54.7 us -> 51.4 us (0.940); the launches traced: 53.9 us -> 51.2 us
  Pallas kernels: 47.3 us -> 44.6 us
    pallas_call x1, Pallas kernels: 47.3 us -> 44.6 us  [fused(): pl.pallas_call(functools.partial(kernel, nf, nz, group, float((count * nd...]
where the time goes in v3:
time: 51.4 us; the launch traced here: 51.2 us
  Pallas kernels  44.6 us (87%)
  local copies, waits for them, and re-layouts  4.52 us (9%)
  other arithmetic  1.35 us (3%)
  between operations  0.68 us (1%)
    pallas_call x1, Pallas kernels, fused(): pl.pallas_call(functools.partial(kernel, nf, nz, group, float((count * nd...  44.6 us
    unnamed x9, local copies, waits for them, and re-layouts  2.33 us
    pallas_call x1, local copies, waits for them, and re-layouts, fused(): pl.pallas_call(functools.partial(kernel, nf, nz, group, float((count * nd...  1.19 us

profile of v3, /device:TPU:0, one launch (start us, length us, event | category | flops | bytes accessed | tf_op | source)
XLA Modules:
  0.0 51.2 jit_solution(3025243795986013164)
XLA Ops:
  0.6 0.8 %copy.14.pat = s32[24,3]{1,0:T(8,128)S(1)} copy(s32[24,3]{0,1:T(4,128)} %param.6) | data formatting | bytes 576 | tf_op args[2]
  1.4 0.0 copy-start.2
  1.4 0.1 eq.15
  1.5 0.1 pad_add_fusion
  1.6 0.8 %select_reduce_fusion = s32[96]{0:T(128)S(1)} fusion(s32[96]{0:T(128)} %constant.1.clone.1, s32[96]{0:T(128)S(1)} %pad_add_fusion, s32[72]{0:T(128)S(1)} %eq.15), kind=kLoop, calls=%fused_computation | loop fusion | flops 34464 | bytes 1440 | tf_op jit(solution)/shard_map/reduce_max | solution.py:337
  2.3 0.5 %compare_select_fusion.prev = s32[96]{0:T(128)} fusion(s32[96]{0:T(128)S(1)} %select_reduce_fusion), kind=kLoop, calls=%fused_computation.3 | loop fusion | flops 192 | bytes 768 | tf_op jit(solution)/shard_map/jit(_where)/select_n | solution.py:338
  2.8 0.0 copy-done.2
  2.9 44.6 %shard_map.67 = (bf16[128,3072]{1,0:T(8,128)(2,1)}, bf16[128,768]{1,0:T(8,128)(2,1)}, f32[24,3,16,128]{3,2,1,0:T(8,128)}) custom-call(s32[24,3]{1,0:T(8,128)} %copy-done.2, s32[96]{0:T(128)} %compare_select_fusion.prev, bf16[128,768]{1,0:T(8,128)(2,1)} %tok.1, bf16[24,3,128,128]{3,2,1,0:T(8,128)(2,1)} %w_hbm.1, bf16[128,3072]{1,0:T(8,128)(2,1)} %g_hbm.1), custom_call_target="tpu_custom_call" | custom-call | tf_op jit(solution)/shard_map/pallas_call | solution.py:344
  47.5 0.0 copy-start
  47.5 0.0 copy-start.1
  47.5 1.2 %copy.15 = f32[24,3,16,128]{3,2,0,1:T(8,128)S(1)} copy(f32[24,3,16,128]{3,2,1,0:T(8,128)} %get-tuple-element.8) | data formatting | bytes 1179648 | tf_op jit(solution)/shard_map/pallas_call | solution.py:344
  48.7 0.9 %reshape.13 = f32[24,3,2048]{2,0,1:T(8,128)} reshape(f32[24,3,16,128]{3,2,0,1:T(8,128)S(1)} %copy.15) | data formatting | bytes 1179648 | tf_op jit(solution)/shard_map/reshape | solution.py:383
  49.6 0.0 copy-done
  49.6 0.9 %copy.18 = bf16[128,3072]{1,0:T(8,128)(2,1)} copy(bf16[128,3072]{1,0:T(8,128)(2,1)S(1)} %copy-done) | data formatting | bytes 1572864
  50.5 0.0 copy-done.1
  50.5 0.7 %copy.19 = bf16[128,768]{1,0:T(8,128)(2,1)} copy(bf16[128,768]{1,0:T(8,128)(2,1)S(1)} %copy-done.1) | data formatting | bytes 393216
  (1 shorter events, 0.0 us)
Async XLA Ops:
  1.4 1.4 %copy-start.2 = (s32[24,3]{1,0:T(8,128)}, s32[24,3]{1,0:T(8,128)S(1)}, u32[]{:S(2)}) copy-start(s32[24,3]{1,0:T(8,128)S(1)} %copy.14.pat) | copy-start | bytes 868
  47.5 2.1 %copy-start = (bf16[128,3072]{1,0:T(8,128)(2,1)S(1)}, bf16[128,3072]{1,0:T(8,128)(2,1)}, u32[]{:S(2)}) copy-start(bf16[128,3072]{1,0:T(8,128)(2,1)} %get-tuple-element.15) | copy-start | bytes 2359300
  47.5 3.0 %copy-start.1 = (bf16[128,768]{1,0:T(8,128)(2,1)S(1)}, bf16[128,768]{1,0:T(8,128)(2,1)}, u32[]{:S(2)}) copy-start(bf16[128,768]{1,0:T(8,128)(2,1)} %get-tuple-element.16) | copy-start | bytes 589828
